TPU v7x, 512 devices: a whole 4x4x16 slice. The times are simulated.
512 devices in a mesh: ka: 8 (over x, core), pts: 64 (over z, y).
Axes of the slice: x: 4, y: 4, z: 16, core: 2. Of those that a mesh axis runs over, the one named last changes fastest.
Arguments:
- orbitals: bfloat16 [216, 2, 4096, 384], P('ka', None, 'pts'), may hold values from -1.5 to 1.5
- counts: int32 [216], P('ka'), may hold values from 60 to 300
- occupation: float32 [216, 384], P('ka'), may hold values from 0.2 to 1
- coulomb: bfloat16 [216, 2, 64, 4096], P('ka', None, None, 'pts'), may hold values from -24 to 24
Outputs:
- exchange_block: bfloat16 [216, 2, 64, 4096], P('ka', None, None, 'pts')
Inputs may be any that keep to these rules, and one draw needn't show every extreme that they name: `counts`: between 60 and 300 occupied bands per k-point.
All inputs are finite; a program needn't handle non-finite values.
Results may differ from a plain program's by a relative error of at most 0.0057.
Values may be sent and summed in bfloat16 or wider, within the bound.
A program may use at most 64 MiB of HBM per device.

v0:
```python
import jax
import jax.numpy as jnp
from jax import lax
from jax.sharding import Mesh
from jax.sharding import PartitionSpec as P

KSIDE = 6
ROW_DEV = 1
PTS = ("pts_0", "pts_1")
KA = ("ka_0", "ka_1")


def gather_axes(array, axes, dim):
    for axis in reversed(axes):
        array = lax.all_gather(array, axis, axis=dim, tiled=True)
    return array


def split_up(array, dim, devices):
    before, after = (array.shape[:dim], array.shape[dim + 1 :])
    return jnp.moveaxis(array.reshape(*before, devices, -1, *after), dim, 0)


def in_order(parts, dim):
    parts = jnp.moveaxis(parts, 0, dim)
    dims = parts.shape
    return parts.reshape(*dims[:dim], dims[dim] * dims[dim + 1], *dims[dim + 2 :])


def moved_by_axis(parts, axes, turns):
    inside = parts.shape[1:]
    whole = parts.reshape(*(lax.axis_size(a) for a in axes), *inside)
    for k in turns:
        whole = lax.all_to_all(whole, axes[k], k, k, tiled=True)
    return whole.reshape(-1, *inside)


def exchange_by_axis(array, axes, turns, split_dim, concat_dim):
    parts = split_up(array, split_dim, lax.axis_size(axes))
    return in_order(moved_by_axis(parts, axes, turns), concat_dim)


def band_gram(left, right):

    def product(first, second):
        return jnp.einsum("krb,knb->krn", first, second, preferred_element_type=jnp.float32)

    real = product(left[:, 0], right[:, 0]) + product(left[:, 1], right[:, 1])
    imag = product(left[:, 1], right[:, 0]) - product(left[:, 0], right[:, 1])
    return jnp.stack([real, imag], 1)


def side_table(sign):
    index = jnp.arange(KSIDE, dtype=jnp.int32)
    phase = index[:, None] * index[None, :] % KSIDE
    angle = phase.astype(jnp.float32) * (2.0 * jnp.pi / KSIDE)
    cosine = jnp.cos(angle)
    sine = jnp.sin(angle) * sign
    top = jnp.stack([cosine, sine], 2)
    bottom = jnp.stack([-sine, cosine], 2)
    return jnp.stack([top, bottom], 1)


def mesh_transform(values, sign):
    table = side_table(sign)
    forms = ["acbd,bxydm->axycm", "acbd,xbydm->xaycm", "acbd,xybdm->xyacm"]
    for form in forms:
        values = jnp.einsum(
            form, table, values, precision=lax.Precision.HIGHEST, preferred_element_type=jnp.float32
        )
    return values


def convolve(density, kernel):
    shape = density.shape
    count = shape[0]
    dens = mesh_transform(density.astype(jnp.float32).reshape(KSIDE, KSIDE, KSIDE, 2, -1), 1.0)
    kern = mesh_transform(kernel.astype(jnp.float32).reshape(KSIDE, KSIDE, KSIDE, 2, -1), 1.0)
    prod_re = kern[:, :, :, 0] * dens[:, :, :, 0] - kern[:, :, :, 1] * dens[:, :, :, 1]
    prod_im = kern[:, :, :, 0] * dens[:, :, :, 1] + kern[:, :, :, 1] * dens[:, :, :, 0]
    back = mesh_transform(jnp.stack([prod_re, prod_im], 3), -1.0)
    scale = -1.0 / (count * count)
    return (back * scale).reshape(shape).astype(jnp.bfloat16)


def local(orbitals, counts, occupation, coulomb):
    slots = orbitals.shape[3]
    band = jnp.arange(slots, dtype=jnp.int32)
    weights = jnp.where(band[None, :] < counts[:, None], occupation, jnp.float32(0.0))
    weighted = (orbitals[:, :, :ROW_DEV, :].astype(jnp.float32) * weights[:, None, None, :]).astype(
        jnp.bfloat16
    )
    gathered = gather_axes(weighted, PTS, 2)
    density = band_gram(gathered, orbitals).astype(jnp.bfloat16)
    result = convolve(
        lax.all_to_all(density, KA, split_axis=3, concat_axis=0, tiled=True),
        lax.all_to_all(coulomb, KA, split_axis=3, concat_axis=0, tiled=True),
    )
    return exchange_by_axis(result, KA, (1, 0), 0, 3)


def solution(mesh):
    finer = Mesh(mesh.devices.reshape(4, 2, 16, 4), ("ka_0", "ka_1", "pts_0", "pts_1"))
    in_specs = (P(KA, None, PTS, None), P(KA), P(KA, None), P(KA, None, None, PTS))
    out_specs = P(KA, None, None, PTS)
    return jax.shard_map(local, mesh=finer, in_specs=in_specs, out_specs=out_specs, check_vma=False)
```

profile of v0, /device:TPU:1, one launch (start us, length us, event | category | flops | bytes accessed | tf_op | source)
XLA Modules:
  0.0 193.9 jit_solution(1851961340840522494)
XLA Ops:
  6.5 1.0 slice.36
  7.6 0.9 fusion.43
  8.5 11.3 %all_gather.6 = bf16[27,2,4,384]{3,1,0,2:T(2,128)(2,1)} all-gather(bf16[27,2,1,384]{3,1,0,2:T(2,128)(2,1)S(1)} %multiply_convert_fusion), channel_id=1, replica_groups=mesh['ka_0'=4,'ka_1'=2,'pts_0'=16,'pts_1'=4] {'pts_1'}, dimensions={2}, use_global_device_ids=true | all-gather | bytes 207360 | tf_op jit(solution)/shard_map/all_gather | solution.py:15
  19.8 2.4 %copy.57 = bf16[27,2,64,64]{2,1,0,3:T(2,128)(2,1)S(1)} copy(bf16[27,2,64,64]{3,2,1,0:T(8,128)(2,1)} %param.7) | data formatting | bytes 884736 | tf_op args[3]
  22.2 1.3 reshape.130
  23.5 11.8 %all-to-all-start = ((bf16[8,2,13824]{2,1,0:T(2,128)(2,1)}), bf16[8,2,13824]{2,1,0:T(2,128)(2,1)S(1)}, u32[]{:S(2)}, u32[]{:S(2)}) async-start(bf16[8,2,13824]{2,1,0:T(2,128)(2,1)} %reshape.130), calls=%async_computation | async-start | bytes 884736 | tf_op jit(solution)/shard_map/all_to_all | solution.py:97
  35.7 8.2 %all-to-all-done = bf16[8,2,13824]{2,1,0:T(2,128)(2,1)S(1)} async-done(((bf16[8,2,13824]{2,1,0:T(2,128)(2,1)}), bf16[8,2,13824]{2,1,0:T(2,128)(2,1)S(1)}, u32[]{:S(2)}, u32[]{:S(2)}) %all-to-all-start) | async-done | bytes 442400 | tf_op jit(solution)/shard_map/all_to_all | solution.py:97
  44.7 4.8 %copy.59 = bf16[8,27,2,64,8]{4,3,2,1,0:T(8,128)(2,1)} copy(bf16[8,27,2,64,8]{3,4,0,2,1:T(8,128)(2,1)S(1)} %bitcast.175) | data formatting | bytes 884736 | tf_op jit(solution)/shard_map/all_to_all | solution.py:97
  49.5 9.7 %reshape.104 = bf16[6,6,6,2,512]{4,3,2,1,0:T(2,128)(2,1)S(1)} reshape(bf16[8,27,2,64,8]{4,3,2,1,0:T(8,128)(2,1)} %copy.59) | data formatting | bytes 884736 | tf_op jit(solution)/shard_map/reshape | solution.py:78
  59.2 1.1 convolution_bitcast_fusion.8
  60.3 32.4 %all-gather.2.cloned.1.call-done = bf16[27,2,64,384]{3,1,0,2:T(2,128)(2,1)} async-done(((bf16[27,2,4,384]{3,1,0,2:T(2,128)(2,1)}), bf16[27,2,64,384]{3,1,0,2:T(2,128)(2,1)}) %all-gather.2.cloned.1.call-update) | async-done | bytes 2654224 | tf_op jit(solution)/shard_map/all_gather | solution.py:15
  92.7 6.9 %fusion.63 = (bf16[27,1,64,384]{3,1,0,2:T(2,128)(2,1)S(1)}, bf16[27,1,64,384]{3,1,0,2:T(2,128)(2,1)S(1)}) fusion(bf16[27,2,64,384]{3,1,0,2:T(2,128)(2,1)} %all-gather.2.cloned.1.call-done), kind=kLoop, calls=%fused_computation.79 | loop fusion | bytes 5308416 | tf_op jit(solution)/shard_map/slice | solution.py:48
  102.3 0.8 copy.68
  103.1 1.3 reshape.128
  104.4 14.1 %all-to-all-start.1 = ((bf16[8,2,13824]{2,1,0:T(2,128)(2,1)}), bf16[8,2,13824]{2,1,0:T(2,128)(2,1)S(1)}, u32[]{:S(2)}, u32[]{:S(2)}) async-start(bf16[8,2,13824]{2,1,0:T(2,128)(2,1)} %reshape.128), calls=%async_computation.1 | async-start | bytes 884736 | tf_op jit(solution)/shard_map/all_to_all | solution.py:96
  118.5 1.9 convolution_bitcast_fusion.6
  120.5 1.8 convolution_bitcast_fusion.5
  122.2 4.9 %all-to-all-done.1 = bf16[8,2,13824]{2,1,0:T(2,128)(2,1)S(1)} async-done(((bf16[8,2,13824]{2,1,0:T(2,128)(2,1)}), bf16[8,2,13824]{2,1,0:T(2,128)(2,1)S(1)}, u32[]{:S(2)}, u32[]{:S(2)}) %all-to-all-start.1) | async-done | bytes 442400 | tf_op jit(solution)/shard_map/all_to_all | solution.py:96
  127.9 4.8 %copy.70 = bf16[8,27,2,64,8]{4,3,2,1,0:T(8,128)(2,1)} copy(bf16[8,27,2,64,8]{3,4,0,2,1:T(8,128)(2,1)S(1)} %bitcast.176) | data formatting | bytes 884736 | tf_op jit(solution)/shard_map/all_to_all | solution.py:96
  132.7 9.7 %reshape.105 = bf16[6,6,6,2,512]{4,3,2,1,0:T(2,128)(2,1)S(1)} reshape(bf16[8,27,2,64,8]{4,3,2,1,0:T(8,128)(2,1)} %copy.70) | data formatting | bytes 884736 | tf_op jit(solution)/shard_map/reshape | solution.py:77
  142.4 0.8 convolution_bitcast_fusion.7
  143.2 1.9 convolution_bitcast_fusion.4
  145.1 1.8 convolution_bitcast_fusion.3
  147.3 1.8 convolution_bitcast_fusion.2
  149.1 1.9 convolution_bitcast_fusion.1
  151.0 1.7 fusion.22
  153.0 9.4 %convert_element_type.66 = bf16[4,2,27,2,64,8]{5,4,3,2,1,0:T(8,128)(2,1)} reshape(bf16[6,6,6,2,512]{4,3,2,1,0:T(2,128)(2,1)S(1)} %copy.79) | data formatting | bytes 884736 | tf_op jit(solution)/shard_map/convert_element_type | solution.py:83
  162.4 5.5 %copy.80 = bf16[4,2,27,2,64,8]{4,5,3,2,0,1:T(8,128)(2,1)S(1)} copy(bf16[4,2,27,2,64,8]{5,4,3,2,1,0:T(8,128)(2,1)} %convert_element_type.66) | data formatting | bytes 884736 | tf_op jit(solution)/shard_map/convert_element_type | solution.py:83
  168.0 0.8 reshape.132
  168.7 4.6 %all_to_all.40 = bf16[2,2,55296]{2,1,0:T(2,128)(2,1)S(1)} all-to-all(bf16[2,2,55296]{2,1,0:T(2,128)(2,1)S(1)} %reshape.132), channel_id=1, replica_groups=mesh['ka_0'=4,'ka_1'=2,'pts_0'=16,'pts_1'=4] {'ka_1'}, dimensions={0} | all-to-all | bytes 884736 | tf_op jit(solution)/shard_map/all_to_all | solution.py:34
  174.6 10.4 %all_to_all.41 = bf16[4,2,27648]{2,1,0:T(2,128)(2,1)S(1)} all-to-all(bf16[4,2,27648]{2,1,0:T(2,128)(2,1)S(1)} %reshape.134), channel_id=1, replica_groups=mesh['ka_0'=4,'ka_1'=2,'pts_0'=16,'pts_1'=4] {'ka_0'}, dimensions={0} | all-to-all | bytes 884736 | tf_op jit(solution)/shard_map/all_to_all | solution.py:34
  185.8 1.2 copy.83
  (30 shorter events, 7.4 us)
Async XLA Ops:
  6.5 86.2 %all-gather.2.cloned.1.call-start = ((), (), s32[]{:S(2)}) async-start(), calls=%async_computation.4 | async-start | bytes 2820096 | tf_op jit(solution)/shard_map/all_gather | solution.py:15
  23.5 20.4 %all-to-all-start = ((bf16[8,2,13824]{2,1,0:T(2,128)(2,1)}), bf16[8,2,13824]{2,1,0:T(2,128)(2,1)S(1)}, u32[]{:S(2)}, u32[]{:S(2)}) async-start(bf16[8,2,13824]{2,1,0:T(2,128)(2,1)} %reshape.130), calls=%async_computation | async-start | bytes 884736 | tf_op jit(solution)/shard_map/all_to_all | solution.py:97
  92.7 6.9 %copy-start = (bf16[27,2,64,384]{3,2,1,0:T(8,128)(2,1)S(1)}, bf16[27,2,64,384]{3,2,1,0:T(8,128)(2,1)}, u32[]{:S(2)}) copy-start(bf16[27,2,64,384]{3,2,1,0:T(8,128)(2,1)} %param.4) | copy-start | bytes 7962628
  104.4 22.7 %all-to-all-start.1 = ((bf16[8,2,13824]{2,1,0:T(2,128)(2,1)}), bf16[8,2,13824]{2,1,0:T(2,128)(2,1)S(1)}, u32[]{:S(2)}, u32[]{:S(2)}) async-start(bf16[8,2,13824]{2,1,0:T(2,128)(2,1)} %reshape.128), calls=%async_computation.1 | async-start | bytes 884736 | tf_op jit(solution)/shard_map/all_to_all | solution.py:96
Sparse Core Ops, SparseCore 0:
  19.9 72.7 all-gather.1
where the time goes:
time: 195 us; the launch traced here: 194 us
  local copies, waits for them, and re-layouts  63.6 us (33%)
  waiting for transfers between devices  45.5 us (23%)
  blocking collectives  26.3 us (13%)
  starting transfers between devices  25.9 us (13%)
  matrix products  17.1 us (9%)
  between operations  13.7 us (7%)
    all_gather x1, waiting for transfers between devices, gather_axes(): array = lax.all_gather(array, axis, axis=dim, tiled=True)  32.4 us
    convert_element_type x3, local copies, waits for them, and re-layouts, convolve(): return (back * scale).reshape(shape).astype(jnp.bfloat16)  15.3 us
    all_to_all x2, blocking collectives, moved_by_axis(): whole = lax.all_to_all(whole, axes[k], k, k, tiled=True)  15 us
    dot_general x9, matrix products, mesh_transform(): jnp.einsum(form, table, values, precision=lax.Precision.HIGHEST, preferre...  14.7 us
    all_to_all x1, starting transfers between devices, local(): lax.all_to_all(density, KA, split_axis=3, concat_axis=0, tiled=True)  14.1 us
    all_to_all x1, starting transfers between devices, local(): lax.all_to_all(coulomb, KA, split_axis=3, concat_axis=0, tiled=True)  11.8 us
    all_gather x1, blocking collectives, gather_axes(): array = lax.all_gather(array, axis, axis=dim, tiled=True)  11.3 us
    reshape x1, local copies, waits for them, and re-layouts, convolve(): kernel.astype(jnp.float32).reshape(KSIDE, KSIDE, KSIDE, 2, -1)  9.7 us
  transfers between devices with their start and end apart: 3, of which 3 were waited for; matrix products, arithmetic and copies ran while one was open for 12% of the time, Pallas kernels for 0%

commit v1 on v0

v1 whole, which is shorter than its diff:
```python
import functools

import jax
import jax.numpy as jnp
import numpy as np
from jax import lax
from jax.experimental import pallas as pl
from jax.experimental.pallas import tpu as pltpu
from jax.sharding import Mesh
from jax.sharding import PartitionSpec as P

KSIDE = 6
PTS = ("pts_0", "pts_1")
KA = ("ka_0", "ka_1")
MESH = pl.DeviceIdType.MESH

NKD = 27
KP = 32
NA = 18
NB = NKD - NA
PLANES = 5
RA = 96
RB = 48
RD = RA + RB
LANES = 128
HALF = 64
ROOT = float(np.sqrt(3.0) / 2.0)


def transform_table():
    index = np.arange(KSIDE**3)
    xyz = np.stack([index // 36, index // 6 % 6, index % 6], 1)
    phase = (xyz @ xyz.T) % KSIDE
    cosine = np.array([1.0, 0.5, -0.5, -1.0, -0.5, 0.5])[phase]
    sine = np.array([0.0, 1.0, 1.0, 0.0, -1.0, -1.0])[phase]
    place = index // NKD * KP + index % NKD
    table = np.zeros((2, 8 * KP, 8 * KP), np.float32)
    table[0][np.ix_(place, place)] = cosine
    table[1][np.ix_(place, place)] = sine
    return table.reshape(2 * 8 * KP, 8 * KP)


def kernel(
    orb_hbm, counts_ref, occ_ref, cou_hbm, table_ref, out_ref,
    orb, cou, right, gath, spread, wide, dense, vsend, vrecv, vhat_a, vhat_b, dsend, drecv, osend, orecv,
    in_sem, s1, r1, s2, r2, s3a, r3a, s3b, r3b, sx, rx,
):
    z0, y0 = lax.axis_index("pts_0"), lax.axis_index("pts_1")
    a0 = lax.axis_index("ka_0") * 2 + lax.axis_index("ka_1")
    zq0, zr0 = z0 // 4, lax.rem(z0, 4)

    def zdev(d):
        return {"pts_0": lax.rem(z0 + d + 16, 16)}

    def ydev(d):
        return {"pts_1": lax.rem(y0 + d, 4)}

    def adev(d):
        a = lax.rem(a0 + d, 8)
        return {"ka_0": a // 2, "ka_1": lax.rem(a, 2)}

    load_orb = pltpu.make_async_copy(orb_hbm, orb, in_sem.at[0])
    load_cou = pltpu.make_async_copy(cou_hbm, cou, in_sem.at[1])
    load_orb.start()
    load_cou.start()

    barrier = pltpu.get_barrier_semaphore()
    peers = [zdev(d) for d in (8, 4, -4, 2, -2, 1, -1)] + [ydev(d) for d in (1, 2, 3)] + [adev(d) for d in range(1, 8)]
    for peer in peers:
        pl.semaphore_signal(barrier, inc=1, device_id=peer, device_id_type=MESH)

    lane = lax.broadcasted_iota(jnp.int32, (1, LANES), 1)
    low = lane < HALF
    plus = jnp.where(low, 1.0, -1.0).astype(jnp.float32)

    def swap(x):
        return pltpu.roll(x, HALF, 1)

    square = (NKD, NKD)
    on = lax.broadcasted_iota(jnp.int32, square, 0) == lax.broadcasted_iota(jnp.int32, square, 1)
    counts = jnp.sum(jnp.where(on, counts_ref[...].astype(jnp.float32), 0.0), axis=1, keepdims=True)
    band = lax.broadcasted_iota(jnp.int32, (NKD, 3 * LANES), 1).astype(jnp.float32)
    weights = jnp.where(band < counts, occ_ref[...], 0.0)

    load_orb.wait()
    for k in range(NKD):
        for c in range(2):
            wide[c * KP + k : c * KP + k + 1, :] = orb[k, c, 0:1, :].astype(jnp.float32) * weights[k : k + 1, :]
    parts = []
    for c in range(2):
        parts.append(wide[c * KP : c * KP + NKD, :])
    rest = jnp.where(low, parts[0][:, 256:], swap(parts[1][:, 256:]))
    planes = [parts[0][:, :128], parts[1][:, :128], parts[0][:, 128:256], parts[1][:, 128:256], rest]
    lead = jnp.concatenate([p[:NA] for p in planes] + [jnp.zeros((RA - PLANES * NA, LANES), jnp.float32)], 0)
    tail = jnp.concatenate([p[NA:] for p in planes] + [jnp.zeros((RB - PLANES * NB, LANES), jnp.float32)], 0)
    gath[zr0, zq0, y0, 0:RA, :] = lead.astype(jnp.bfloat16)
    gath[zr0, zq0, y0, RA:RD, :] = tail.astype(jnp.bfloat16)

    pl.semaphore_wait(barrier, len(peers))

    def send(src, dst, ssem, rsem, peer):
        return pltpu.make_async_remote_copy(
            src_ref=src, dst_ref=dst, send_sem=ssem, recv_sem=rsem, device_id=peer, device_id_type=MESH
        )

    sent = []

    def go(copy):
        copy.start()
        sent.append(copy)

    def first(i, zq):
        ref = gath.at[zr0, zq, y0]
        return send(ref, ref, s1.at[i], r1.at[i], zdev((4, -4, 8)[i]))

    def side(zr, y, rows, i, send_sem, recv_sem):
        part = (pl.ds(0, 4), pl.ds(0, 4), pl.ds(0, 2), pl.ds(2, 2))[i]
        ref = gath.at[zr, part, y, rows]
        return send(ref, ref, send_sem, recv_sem, zdev((1, -1, 2, -2)[i]))

    def across(zr, y, rows, j, send_sem, recv_sem):
        ref = gath.at[zr, :, y, rows]
        return send(ref, ref, send_sem, recv_sem, ydev((1, 3, 2)[j]))

    rows_a, rows_b = pl.ds(0, RA), pl.ds(RA, RB)
    from_z = (3, 1, 2, 2)
    from_y = (3, 1, 2)

    def res(d):
        return lax.rem(zr0 + d, 4)

    def yy(d):
        return lax.rem(y0 + d, 4)

    def scatter(zr, y, rows, base, zqs):
        def one(zq, carry):
            r = (zq * 4 + zr) * 4 + y
            block = gath[zr, zq, y, rows, :].astype(jnp.float32)
            spread[pl.ds(base * 64 + r, rows.size, stride=64), :] = block
            return carry

        lax.fori_loop(zqs[0], zqs[1], one, 0)

    def scatter_a(zr, y):
        scatter(zr, y, rows_a, 0, (0, 4))

    def scatter_b(zr, y, zqs=(0, 4)):
        scatter(zr, y, rows_b, RA, zqs)

    for i in (2, 0, 1):
        go(first(i, zq0))

    load_cou.wait()
    for k in range(NKD, KP):
        wide_rows = pl.ds(k, 64, stride=KP)
        vhat_a[wide_rows, :] = jnp.zeros((64, LANES), jnp.float32)

    def lay(k, carry):
        pair = jnp.concatenate([cou[k, 0], cou[k, 1]], axis=1).astype(jnp.float32)
        vhat_a[pl.ds(k, 64, stride=KP), :] = pair
        return carry

    lax.fori_loop(0, NKD, lay, 0)
    vsend[...] = vhat_a[...].astype(jnp.bfloat16).reshape(8, 8, KP, LANES)

    def swap_out(stage, src, dst_of, d):
        return send(src, dst_of, sx.at[stage, d - 1], rx.at[stage, d - 1], adev(d))

    def to_mine(stage, buffer, landing, d):
        return swap_out(stage, buffer.at[lax.rem(a0 + d, 8)], landing.at[:, a0], d)

    for d in range(1, 8):
        go(to_mine(0, vsend, vrecv, d))
    vrecv[:, a0] = vsend[a0]

    for i, d in ((0, -4), (1, 4), (2, 8)):
        first(i, lax.rem(zq0 + d // 4 + 4, 4)).wait_recv()
    for i in range(4):
        go(side(zr0, y0, rows_a, i, s2.at[i], r2.at[i]))
    for j in range(3):
        go(across(zr0, y0, rows_b, j, s2.at[4 + j], r2.at[4 + j]))
    for j in range(3):
        go(across(zr0, y0, rows_a, j, s3a.at[j, 0], r3a.at[j, 0]))
    for i in range(4):
        go(side(zr0, y0, rows_b, i, s3b.at[i, 0], r3b.at[i, 0]))
    scatter_a(zr0, y0)
    scatter_b(zr0, y0)

    def turn(k, carry):
        re, im = orb[k, 0], orb[k, 1]
        minus = -im
        rest_re = jnp.where(low, re[:, 256:].astype(jnp.float32), swap(im[:, 256:].astype(jnp.float32)))
        rest_im = jnp.where(low, minus[:, 256:].astype(jnp.float32), swap(re[:, 256:].astype(jnp.float32)))
        right[k, 0:64, :] = jnp.concatenate(
            [re[:, :128], im[:, :128], re[:, 128:256], im[:, 128:256], rest_re.astype(jnp.bfloat16)], 1
        )
        right[k, 64:128, :] = jnp.concatenate(
            [minus[:, :128], re[:, :128], minus[:, 128:256], re[:, 128:256], rest_im.astype(jnp.bfloat16)], 1
        )
        return carry

    lax.fori_loop(0, NKD, turn, 0)

    groups_z = (((0,), 1), ((1,), 2), ((2, 3), 3))
    for which, order in groups_z:
        for i in which:
            side(res(from_z[i]), y0, rows_a, i, s2.at[i], r2.at[i]).wait_recv()
        for j in range(3):
            go(across(res(from_z[which[0]]), y0, rows_a, j, s3a.at[j, order], r3a.at[j, order]))
        j = order - 1
        across(zr0, yy(from_y[j]), rows_b, j, s2.at[4 + j], r2.at[4 + j]).wait_recv()
        for i in range(4):
            go(side(zr0, yy(from_y[j]), rows_b, i, s3b.at[i, order], r3b.at[i, order]))
    for which, order in groups_z:
        scatter_a(res(from_z[which[0]]), y0)
        scatter_b(zr0, yy(from_y[order - 1]))

    deltas_z = (0,) + tuple(from_z[which[0]] for which, _ in groups_z)
    deltas_y = (0,) + from_y

    def forward(x):
        y = jnp.dot(table_ref[...], x, preferred_element_type=jnp.float32)
        return y[: 8 * KP] + (ROOT * plus) * swap(y[8 * KP :])

    for d in range(1, 8):
        to_mine_from = swap_out(0, vsend.at[0], vrecv.at[:, lax.rem(a0 + 8 - d, 8)], d)
        to_mine_from.wait_recv()

    def kern(r, carry):
        v = forward(vrecv[r].reshape(8 * KP, LANES))
        w = swap(v)
        rows = pl.ds(pl.multiple_of(r * 8 * KP, 8 * KP), 8 * KP)
        vhat_a[rows, :] = jnp.where(low, v, w)
        vhat_b[rows, :] = jnp.where(low, -w, v)
        return carry

    lax.fori_loop(0, 8, kern, 0)

    for order in range(4):
        for j in range(3):
            zr, y = res(deltas_z[order]), yy(from_y[j])
            across(zr, y, rows_a, j, s3a.at[j, order], r3a.at[j, order]).wait_recv()
            scatter_a(zr, y)
        for i in range(4):
            zr, y = res(from_z[i]), yy(deltas_y[order])
            side(zr, y, rows_b, i, s3b.at[i, order], r3b.at[i, order]).wait_recv()
            scatter_b(zr, y, ((0, 4), (0, 4), (0, 2), (2, 4))[i])

    for k in range(NKD, KP):
        dense[pl.ds(k, 64, stride=KP), :] = jnp.zeros((64, LANES), jnp.float32)

    def dens(base, count, start):
        def one(k, carry):
            left = [
                spread[pl.ds(pl.multiple_of((base + j * count + k) * 64, 64), 64), :].astype(jnp.bfloat16)
                for j in range(PLANES)
            ]
            d = lax.dot_general(
                jnp.concatenate(left, 1), right[start + k], (((1,), (1,)), ((), ())), preferred_element_type=jnp.float32
            )
            dense[pl.ds(start + k, 64, stride=KP), :] = d
            return carry

        lax.fori_loop(0, count, one, 0)

    dens(0, NA, 0)
    dens(RA, NB, NA)
    dsend[...] = dense[...].astype(jnp.bfloat16).reshape(8, 8, KP, LANES)
    for d in range(1, 8):
        go(to_mine(1, dsend, drecv, d))
    drecv[:, a0] = dsend[a0]
    for d in range(1, 8):
        swap_out(1, dsend.at[0], drecv.at[:, lax.rem(a0 + 8 - d, 8)], d).wait_recv()

    scale = -1.0 / float(KSIDE**6)

    def conv(r, carry):
        d = forward(drecv[r].reshape(8 * KP, LANES))
        rows = pl.ds(pl.multiple_of(r * 8 * KP, 8 * KP), 8 * KP)
        product = vhat_a[rows, :] * d + vhat_b[rows, :] * swap(d)
        y = jnp.dot(table_ref[...], product.astype(jnp.bfloat16), preferred_element_type=jnp.float32)
        back = scale * y[: 8 * KP] - (scale * ROOT * plus) * swap(y[8 * KP :])
        osend[r] = back.astype(jnp.bfloat16).reshape(8, KP, LANES)
        return carry

    lax.fori_loop(0, 8, conv, 0)

    def home(d):
        mine = pl.ds(pl.multiple_of(a0 * 8, 8), 8)
        return swap_out(2, osend.at[:, lax.rem(a0 + d, 8)], orecv.at[mine], d)

    for d in range(1, 8):
        go(home(d))
    orecv[pl.ds(pl.multiple_of(a0 * 8, 8), 8)] = osend[:, a0]
    for d in range(1, 8):
        theirs = pl.ds(pl.multiple_of(lax.rem(a0 + 8 - d, 8) * 8, 8), 8)
        swap_out(2, osend.at[:, 0], orecv.at[theirs], d).wait_recv()

    def unlay(r, carry):
        spread[pl.ds(r, KP, stride=64), :] = orecv[r].astype(jnp.float32)
        return carry

    lax.fori_loop(0, 64, unlay, 0)

    def finish(k, carry):
        o = spread[pl.ds(pl.multiple_of(k * 64, 64), 64), :]
        out_ref[k, 0] = o[:, :HALF].astype(jnp.bfloat16)
        out_ref[k, 1] = swap(o)[:, :HALF].astype(jnp.bfloat16)
        return carry

    lax.fori_loop(0, NKD, finish, 0)
    for copy in sent:
        copy.wait_send()


def local(orbitals, counts, occupation, coulomb):
    table = jnp.asarray(transform_table(), jnp.bfloat16)
    bf, f32 = jnp.bfloat16, jnp.float32
    vmem = pl.BlockSpec(memory_space=pltpu.VMEM)
    anywhere = pl.BlockSpec(memory_space=pl.ANY)
    dma = pltpu.SemaphoreType.DMA
    return pl.pallas_call(
        kernel,
        out_shape=jax.ShapeDtypeStruct((NKD, 2, 64, 64), bf),
        in_specs=[anywhere, vmem, vmem, anywhere, vmem],
        out_specs=vmem,
        scratch_shapes=[
            pltpu.VMEM((NKD, 2, 64, 384), bf),
            pltpu.VMEM((NKD, 2, 64, 64), bf),
            pltpu.VMEM((NKD, 128, PLANES * LANES), bf),
            pltpu.VMEM((4, 4, 4, RD, LANES), bf),
            pltpu.VMEM((RD * 64, LANES), f32),
            pltpu.VMEM((2 * KP, 384), f32),
            pltpu.VMEM((64 * KP, LANES), f32),
            pltpu.VMEM((8, 8, KP, LANES), bf),
            pltpu.VMEM((8, 8, KP, LANES), bf),
            pltpu.VMEM((64 * KP, LANES), f32),
            pltpu.VMEM((64 * KP, LANES), f32),
            pltpu.VMEM((8, 8, KP, LANES), bf),
            pltpu.VMEM((8, 8, KP, LANES), bf),
            pltpu.VMEM((8, 8, KP, LANES), bf),
            pltpu.VMEM((64, KP, LANES), bf),
            dma((2,)),
            dma((3,)),
            dma((3,)),
            dma((7,)),
            dma((7,)),
            dma((3, 4)),
            dma((3, 4)),
            dma((4, 4)),
            dma((4, 4)),
            dma((3, 7)),
            dma((3, 7)),
        ],
        compiler_params=pltpu.CompilerParams(
            collective_id=0, has_side_effects=True, vmem_limit_bytes=48 * 1024 * 1024
        ),
    )(orbitals, counts.reshape(1, NKD), occupation, coulomb, table)


def solution(mesh):
    finer = Mesh(mesh.devices.reshape(4, 2, 16, 4), ("ka_0", "ka_1", "pts_0", "pts_1"))
    in_specs = (P(KA, None, PTS, None), P(KA), P(KA, None), P(KA, None, None, PTS))
    out_specs = P(KA, None, None, PTS)
    return jax.shard_map(local, mesh=finer, in_specs=in_specs, out_specs=out_specs, check_vma=False)
```

time: 195 us -> 84.7 us (0.43)
  Pallas kernels: 0 us -> 77.3 us
  local copies, waits for them, and re-layouts: 63.6 us -> 6.23 us
  waiting for transfers between devices: 45.5 us -> 0 us
  blocking collectives: 26.3 us -> 0 us
  starting transfers between devices: 25.9 us -> 0 us
  matrix products: 17.1 us -> 0 us
  between operations: 13.7 us -> 0.01 us
    pallas_call x0 -> x1, Pallas kernels: none -> 77.3 us  [local(): pl.pallas_call(kernel, out_shape=jax.ShapeDtypeStruct((NKD, 2, 64, 64), b...]
    all_gather x1 -> x0, waiting for transfers between devices: 32.4 us -> none  [gather_axes(): array = lax.all_gather(array, axis, axis=dim, tiled=True)]
    all_to_all x2 -> x0, starting transfers between devices: 25.9 us -> none  [the longest x1 14.1 us: local(): lax.all_to_all(density, KA, split_axis=3, concat_axis=0, tiled=True)]
    reshape x3 -> x0, local copies, waits for them, and re-layouts: 20.6 us -> none  [the longest x1 9.7 us: convolve(): kernel.astype(jnp.float32).reshape(KSIDE, KSIDE, KSIDE, 2, -1)]
    dot_general x13 -> x0, matrix products: 17.1 us -> none  [the longest x9 14.7 us: mesh_transform(): jnp.einsum(form, table, values, precision=lax.Precision.HIGHEST, preferre...]
    convert_element_type x3 -> x0, local copies, waits for them, and re-layouts: 15.3 us -> none  [convolve(): return (back * scale).reshape(shape).astype(jnp.bfloat16)]
    all_to_all x2 -> x0, blocking collectives: 15 us -> none  [moved_by_axis(): whole = lax.all_to_all(whole, axes[k], k, k, tiled=True)]
    all_to_all x2 -> x0, waiting for transfers between devices: 13.1 us -> none  [the longest x1 8.24 us: local(): lax.all_to_all(coulomb, KA, split_axis=3, concat_axis=0, tiled=True)]
  transfers between devices with their start and end apart: 3 -> 0, of which waited for: 3 -> 0; matrix products, arithmetic and copies ran while one was open for 12% -> 0% of each run, Pallas kernels for 0% -> 0%
where the time goes in v1:
time: 84.7 us; the launch traced here: 83.6 us
  Pallas kernels  77.3 us (91%)
  local copies, waits for them, and re-layouts  6.23 us (7%)
    pallas_call x1, Pallas kernels, local(): pl.pallas_call(kernel, out_shape=jax.ShapeDtypeStruct((NKD, 2, 64, 64), b...  77.3 us
    unnamed x11, local copies, waits for them, and re-layouts  6.23 us

profile of v1, /device:TPU:1, one launch (start us, length us, event | category | flops | bytes accessed | tf_op | source)
XLA Modules:
  0.0 83.6 jit_solution(12994278949833998726)
XLA Ops:
  0.0 0.0 copy-start
  0.0 1.7 %copy-done = bf16[27,2,64,384]{3,2,1,0:T(8,128)(2,1)S(1)} copy-done((bf16[27,2,64,384]{3,2,1,0:T(8,128)(2,1)S(1)}, bf16[27,2,64,384]{3,2,1,0:T(8,128)(2,1)}, u32[]{:S(2)}) %copy-start) | copy-done | bytes 2654232
  1.8 0.0 copy-start.1
  1.8 1.2 %copy-done.1 = bf16[27,2,64,64]{3,2,1,0:T(8,128)(2,1)S(1)} copy-done((bf16[27,2,64,64]{3,2,1,0:T(8,128)(2,1)S(1)}, bf16[27,2,64,64]{3,2,1,0:T(8,128)(2,1)}, u32[]{:S(2)}) %copy-start.1) | copy-done | bytes 442392
  2.9 0.0 copy-start.2
  2.9 0.9 %copy-done.2 = bf16[512,256]{1,0:T(8,128)(2,1)S(1)} copy-done((bf16[512,256]{1,0:T(8,128)(2,1)S(1)}, bf16[512,256]{1,0:T(8,128)(2,1)}, u32[]{:S(2)}) %copy-start.2) | copy-done | bytes 262168
  3.9 0.0 copy-start.3
  3.9 0.8 copy-done.3
  4.7 0.0 copy-start.4
  4.7 0.7 copy-done.4
  5.3 77.3 %shard_map.55 = bf16[27,2,64,64]{3,2,1,0:T(8,128)(2,1)S(1)} custom-call(bf16[27,2,64,384]{3,2,1,0:T(8,128)(2,1)S(1)} %copy-done, s32[1,27]{1,0:T(1,128)S(1)} %bitcast.1, f32[27,384]{1,0:T(8,128)S(1)} %copy-done.3, bf16[27,2,64,64]{3,2,1,0:T(8,128)(2,1)S(1)} %copy-done.1, bf16[512,256]{1,0:T(8,128)(2,1)S(1)} %copy-done.2), custom_call_target="tpu_custom_call" | custom-call | tf_op jit(solution)/shard_map/pallas_call | solution.py:322
  82.6 0.9 %copy.7 = bf16[27,2,64,64]{3,2,1,0:T(8,128)(2,1)} copy(bf16[27,2,64,64]{3,2,1,0:T(8,128)(2,1)S(1)} %shard_map.55) | data formatting | bytes 884736
Async XLA Ops:
  0.0 1.7 %copy-start = (bf16[27,2,64,384]{3,2,1,0:T(8,128)(2,1)S(1)}, bf16[27,2,64,384]{3,2,1,0:T(8,128)(2,1)}, u32[]{:S(2)}) copy-start(bf16[27,2,64,384]{3,2,1,0:T(8,128)(2,1)} %orb_hbm.1) | copy-start | bytes 7962628
  1.8 1.2 %copy-start.1 = (bf16[27,2,64,64]{3,2,1,0:T(8,128)(2,1)S(1)}, bf16[27,2,64,64]{3,2,1,0:T(8,128)(2,1)}, u32[]{:S(2)}) copy-start(bf16[27,2,64,64]{3,2,1,0:T(8,128)(2,1)} %cou_hbm.1) | copy-start | bytes 1327108
  2.9 0.9 %copy-start.2 = (bf16[512,256]{1,0:T(8,128)(2,1)S(1)}, bf16[512,256]{1,0:T(8,128)(2,1)}, u32[]{:S(2)}) copy-start(bf16[512,256]{1,0:T(8,128)(2,1)} %constant.2.clone.table_ref) | copy-start | bytes 786436
  3.9 0.8 copy-start.3
  4.7 0.7 copy-start.4

commit v2 on v0

v2 whole, which is shorter than its diff:
```python
import functools

import jax
import jax.numpy as jnp
import numpy as np
from jax import lax
from jax.experimental import pallas as pl
from jax.experimental.pallas import tpu as pltpu
from jax.sharding import Mesh
from jax.sharding import PartitionSpec as P

KSIDE = 6
PTS = ("pts_0", "pts_1")
KA = ("ka_0", "ka_1")
MESH = pl.DeviceIdType.MESH

NKD = 27
KP = 32
PLANES = 5
RD = 144
LANES = 128
HALF = 64
PTILE = 8 * KP
ROOT = float(np.sqrt(3.0) / 2.0)
SCALE = -1.0 / float(KSIDE**6)

DELTA_Y = (0, 1, 3, 2)
STAGES = ((0, 1), (1, 2), (3, 1))
OFFSETS = (0, -1, 1, -2, 2, -4, 4, -5, 3, -3, 5, -6, 6, 8, 7, -7)
NEAR = {0: (1, -1, 2, -2), -4: (1, -1, 2), 4: (1, -1, -2), 8: (1, -1)}
CUT = 80


def transform_table():
    index = np.arange(KSIDE**3)
    xyz = np.stack([index // 36, index // 6 % 6, index % 6], 1)
    phase = (xyz @ xyz.T) % KSIDE
    cosine = np.array([1.0, 0.5, -0.5, -1.0, -0.5, 0.5])[phase]
    sine = np.array([0.0, 1.0, 1.0, 0.0, -1.0, -1.0])[phase]
    place = index // NKD * KP + index % NKD
    table = np.zeros((2, PTILE, PTILE), np.float32)
    table[0][np.ix_(place, place)] = cosine
    table[1][np.ix_(place, place)] = sine
    return table.reshape(2 * PTILE, PTILE)


def kernel(
    orb_hbm, counts_hbm, occ_hbm, cou_hbm, table_hbm, out_ref,
    row, counts_ref, occ_ref, orb, cou, table_ref,
    right, gath, spread, wide, dense, vsend, vrecv, vhat_a, vhat_b, dsend, drecv, osend, orecv,
    in_sem, sz, rz, sy, ry, sf, rf, sx, rx,
):
    z0, y0 = lax.axis_index("pts_0"), lax.axis_index("pts_1")
    a0 = lax.axis_index("ka_0") * 2 + lax.axis_index("ka_1")

    def zdev(d):
        return {"pts_0": lax.rem(z0 + d + 16, 16)}

    def ydev(d):
        return {"pts_1": lax.rem(y0 + d, 4)}

    def adev(d):
        a = lax.rem(a0 + d, 8)
        return {"ka_0": a // 2, "ka_1": lax.rem(a, 2)}

    def zz(d):
        return lax.rem(z0 + d + 16, 16)

    def yy(d):
        return lax.rem(y0 + d, 4)

    loads = [
        pltpu.make_async_copy(src, dst, in_sem.at[i])
        for i, (src, dst) in enumerate((
            (orb_hbm.at[:, :, 0:16, :], row),
            (counts_hbm, counts_ref),
            (occ_hbm, occ_ref),
            (cou_hbm, cou),
            (orb_hbm, orb),
            (table_hbm, table_ref),
        ))
    ]
    for load in loads:
        load.start()

    barrier = pltpu.get_barrier_semaphore()
    peers = [zdev(d) for d in (4, -4, 2, -2, 1, -1)] + [ydev(d) for d in (1, 3)] + [adev(d) for d in range(1, 8)]
    for peer in peers:
        pl.semaphore_signal(barrier, inc=1, device_id=peer, device_id_type=MESH)

    lane = lax.broadcasted_iota(jnp.int32, (1, LANES), 1)
    low = lane < HALF
    plus = jnp.where(low, 1.0, -1.0).astype(jnp.float32)
    plus2 = jnp.concatenate([plus, plus], 1)
    low2 = jnp.concatenate([lane, lane], 1) < HALF

    def swap(x):
        return pltpu.roll(x, HALF, 1)

    def swap2(x):
        return jnp.concatenate([swap(x[:, :LANES]), swap(x[:, LANES:])], 1)

    for load in loads[:3]:
        load.wait()
    square = (NKD, NKD)
    on = lax.broadcasted_iota(jnp.int32, square, 0) == lax.broadcasted_iota(jnp.int32, square, 1)
    counts = jnp.sum(jnp.where(on, counts_ref[...].astype(jnp.float32), 0.0), axis=1, keepdims=True)
    band = lax.broadcasted_iota(jnp.int32, (NKD, 3 * LANES), 1).astype(jnp.float32)
    weights = jnp.where(band < counts, occ_ref[...], 0.0)
    for k in range(NKD):
        for c in range(2):
            wide[c * KP + k : c * KP + k + 1, :] = row[k, c, 0:1, :].astype(jnp.float32)
    parts = [wide[c * KP : c * KP + NKD, :] * weights for c in range(2)]
    rest = jnp.where(low, parts[0][:, 256:], swap(parts[1][:, 256:]))
    planes = [parts[0][:, :128], parts[1][:, :128], parts[0][:, 128:256], parts[1][:, 128:256], rest]
    block = jnp.concatenate(planes + [jnp.zeros((RD - PLANES * NKD, LANES), jnp.float32)], 0)
    gath[z0, y0] = block.astype(jnp.bfloat16)

    pl.semaphore_wait(barrier, len(peers))

    def send(src, dst, ssem, rsem, peer):
        return pltpu.make_async_remote_copy(
            src_ref=src, dst_ref=dst, send_sem=ssem, recv_sem=rsem, device_id=peer, device_id_type=MESH
        )

    sent = []

    def go(copy):
        copy.start()
        sent.append(copy)

    def along(o, dz):
        ref, to = gath.at[zz(o), y0], (o - dz) % 16
        return send(ref, ref, sz.at[to], rz.at[to], zdev(dz))

    def chain(o):
        rows, to = (pl.ds(0, CUT), 8) if o > 0 else (pl.ds(CUT, RD - CUT), 16)
        ref = gath.at[zz(o), y0, rows]
        return send(ref, ref, sz.at[to], rz.at[to], zdev(-o))

    def chained(o):
        rows, to = (pl.ds(0, CUT), 8) if o > 0 else (pl.ds(CUT, RD - CUT), 16)
        ref = gath.at[zz(8), y0, rows]
        return send(ref, ref, sz.at[to], rz.at[to], zdev(-o))

    def across(i, o, y):
        ref = gath.at[zz(o), y]
        return send(ref, ref, sy.at[i, o % 16], ry.at[i, o % 16], ydev((1, 3)[i]))

    def onward(o, y):
        ref = gath.at[zz(o), y]
        return send(ref, ref, sf.at[o % 16], rf.at[o % 16], ydev((1, 3)[OFFSETS.index(o) % 2]))

    def near(o):
        for dz in NEAR[o]:
            go(along(o, dz))

    def sides(o):
        for i in range(2):
            go(across(i, o, y0))

    def arrive(o):
        ref = gath.at[zz(o), y0]
        send(ref, ref, sz.at[o % 16], rz.at[o % 16], zdev(1)).wait_recv()
        sides(o)

    def pass_on(o):
        for i in range(2):
            across(i, o, yy((3, 1)[i])).wait_recv()
        go(onward(o, yy((3, 1)[OFFSETS.index(o) % 2])))

    sides(0)
    for dz in (4, -4):
        go(along(0, dz))
    near(0)

    loads[3].wait()
    for k in range(NKD, KP):
        dense[pl.ds(k, 64, stride=KP), :] = jnp.zeros((64, LANES), jnp.float32)

    def lay(k, carry):
        pair = jnp.concatenate([cou[k, 0], cou[k, 1]], axis=1).astype(jnp.float32)
        dense[pl.ds(k, 64, stride=KP), :] = pair
        return carry

    lax.fori_loop(0, NKD, lay, 0)
    vsend[...] = dense[...].astype(jnp.bfloat16).reshape(8, 8, KP, LANES)

    def move(stage, src, dst, d):
        return send(src, dst, sx.at[stage, d - 1], rx.at[stage, d - 1], adev(d))

    def theirs(d):
        return lax.rem(a0 + 8 - d, 8)

    for d in range(1, 8):
        go(move(0, vsend.at[lax.rem(a0 + d, 8)], vrecv.at[:, a0], d))
    vrecv[:, a0] = vsend[a0]

    def turn(k, carry):
        re, im = orb[k, 0], orb[k, 1]
        minus = -im
        rest_re = jnp.where(low, re[:, 256:].astype(jnp.float32), swap(im[:, 256:].astype(jnp.float32)))
        rest_im = jnp.where(low, minus[:, 256:].astype(jnp.float32), swap(re[:, 256:].astype(jnp.float32)))
        right[k, 0:64, :] = jnp.concatenate(
            [re[:, :128], im[:, :128], re[:, 128:256], im[:, 128:256], rest_re.astype(jnp.bfloat16)], 1
        )
        right[k, 64:128, :] = jnp.concatenate(
            [minus[:, :128], re[:, :128], minus[:, 128:256], re[:, 128:256], rest_im.astype(jnp.bfloat16)], 1
        )
        return carry

    def scatter(stage, u, o, y):
        first_group, groups = STAGES[stage]
        base, rows = first_group * 16 * RD, groups * 16
        spread[pl.ds(base + u * 16 + zz(o), RD, stride=rows), :] = gath[zz(o), y].astype(jnp.float32)

    def dens(stage, start, stop):
        first_group, groups = STAGES[stage]
        base, rows = first_group * 16 * RD, groups * 16

        def one(k, carry):
            left = [
                spread[pl.ds(pl.multiple_of(base + (j * NKD + k) * rows, 16), rows), :].astype(jnp.bfloat16)
                for j in range(PLANES)
            ]
            d = lax.dot_general(
                jnp.concatenate(left, 1), right[k], (((1,), (1,)), ((), ())), preferred_element_type=jnp.float32
            )
            dense[pl.ds(first_group * 16 * KP + k, rows, stride=KP), :] = d
            return carry

        lax.fori_loop(start, stop, one, 0, unroll=3)

    def hand_over(stage):
        first_group, groups = STAGES[stage]
        for u in range(first_group, first_group + groups):
            d = dense[u * 16 * KP : (u + 1) * 16 * KP, :].astype(jnp.bfloat16)
            dsend[:, 2 * u : 2 * u + 2] = d.reshape(8, 2, KP, LANES)
        part = pl.ds(2 * first_group, 2 * groups)
        for d in range(1, 8):
            go(move(1 + stage, dsend.at[lax.rem(a0 + d, 8), part], drecv.at[part, a0], d))
        drecv[part, a0] = dsend[a0, part]

    def forward(x):
        y = jnp.dot(table_ref[...], x, preferred_element_type=jnp.float32)
        return y[:PTILE] + (ROOT * plus2) * swap2(y[PTILE:])

    def pair(ref, i, j):
        return jnp.concatenate([ref[i].reshape(PTILE, LANES), ref[j].reshape(PTILE, LANES)], 1)

    def convolve(stage):
        first_group, groups = STAGES[stage]
        part = pl.ds(2 * first_group, 2 * groups)
        for d in range(1, 8):
            move(1 + stage, dsend.at[0, part], drecv.at[part, theirs(d)], d).wait_recv()
        for u in range(first_group, first_group + groups):
            d = forward(pair(drecv, 2 * u, 2 * u + 1))
            y = yy(DELTA_Y[u])
            product = vhat_a[y] * d + vhat_b[y] * swap2(d)
            t = jnp.dot(table_ref[...], product.astype(jnp.bfloat16), preferred_element_type=jnp.float32)
            back = SCALE * t[:PTILE] - (SCALE * ROOT * plus2) * swap2(t[PTILE:])
            back = back.astype(jnp.bfloat16)
            osend[2 * u] = back[:, :LANES].reshape(8, KP, LANES)
            osend[2 * u + 1] = back[:, LANES:].reshape(8, KP, LANES)
        for d in range(1, 8):
            go(move(4 + stage, osend.at[part, lax.rem(a0 + d, 8)], orecv.at[a0, part], d))
        orecv[a0, part] = osend[part, a0]

    def unlay(stage):
        first_group, groups = STAGES[stage]
        part = pl.ds(2 * first_group, 2 * groups)
        for d in range(1, 8):
            move(4 + stage, osend.at[part, 0], orecv.at[theirs(d), part], d).wait_recv()

        def one(a, carry):
            for u in range(first_group, first_group + groups):
                for i in range(2):
                    r = (2 * a + i) * 4 + yy(DELTA_Y[u])
                    spread[pl.ds(r, KP, stride=64), :] = orecv[a, 2 * u + i].astype(jnp.float32)
            return carry

        lax.fori_loop(0, 8, one, 0)

    for o in (-1, 1, -2, 2):
        arrive(o)
    pass_on(0)
    for o in (-4, 4):
        arrive(o)
        go(chain(o))
        near(o)
    loads[4].wait()
    lax.fori_loop(0, 9, turn, 0)
    for o in (-5, 3, -3, 5, -6, 6):
        arrive(o)
    for o in (-1, 1, -2, 2):
        pass_on(o)
    for o in (4, -4):
        chained(o).wait_recv()
    sides(8)
    near(8)
    lax.fori_loop(9, 18, turn, 0)
    for o in (-4, 4):
        pass_on(o)
    for o in (7, -7):
        arrive(o)
    lax.fori_loop(18, NKD, turn, 0)
    for o in OFFSETS[:8]:
        scatter(0, 0, o, y0)
    for o in (-5, 3, -3):
        pass_on(o)
    for o in OFFSETS[8:]:
        scatter(0, 0, o, y0)
    for o in (5, -6, 6):
        pass_on(o)
    for k in range(NKD, KP):
        dense[pl.ds(k, 64, stride=KP), :] = jnp.zeros((64, LANES), jnp.float32)
    dens(0, 0, NKD)
    hand_over(0)
    for o in (8, 7, -7):
        pass_on(o)

    loads[5].wait()
    for d in range(1, 8):
        move(0, vsend.at[0], vrecv.at[:, theirs(d)], d).wait_recv()

    def kern(y):
        v = forward(pair(vrecv, y, y + 4))
        w = swap2(v)
        vhat_a[y] = jnp.where(low2, v, w)
        vhat_b[y] = jnp.where(low2, -w, v)

    for y in range(4):
        kern(y)
    for o in OFFSETS:
        for u in range(2):
            scatter(1, u, o, yy((1, 3)[u]))
    dens(1, 0, NKD)
    hand_over(1)
    convolve(0)
    for o in OFFSETS:
        onward(o, yy(2)).wait_recv()
        scatter(2, 0, o, yy(2))
    dens(2, 0, NKD)
    hand_over(2)
    convolve(1)
    unlay(0)
    convolve(2)
    unlay(1)
    unlay(2)

    def finish(k, carry):
        o = spread[pl.ds(pl.multiple_of(k * 64, 64), 64), :]
        out_ref[k, 0] = o[:, :HALF].astype(jnp.bfloat16)
        out_ref[k, 1] = swap(o)[:, :HALF].astype(jnp.bfloat16)
        return carry

    lax.fori_loop(0, NKD, finish, 0)
    for copy in sent:
        copy.wait_send()


def local(orbitals, counts, occupation, coulomb):
    table = jnp.asarray(transform_table(), jnp.bfloat16)
    bf, f32 = jnp.bfloat16, jnp.float32
    vmem = pltpu.VMEM
    dma = pltpu.SemaphoreType.DMA
    return pl.pallas_call(
        kernel,
        out_shape=jax.ShapeDtypeStruct((NKD, 2, 64, 64), bf),
        in_specs=[pl.BlockSpec(memory_space=pltpu.HBM)] * 5,
        out_specs=pl.BlockSpec(memory_space=vmem),
        scratch_shapes=[
            vmem((NKD, 2, 16, 384), bf),
            vmem((1, NKD), jnp.int32),
            vmem((NKD, 384), f32),
            vmem((NKD, 2, 64, 384), bf),
            vmem((NKD, 2, 64, 64), bf),
            vmem((2 * PTILE, PTILE), bf),
            vmem((NKD, 128, PLANES * LANES), bf),
            vmem((16, 4, RD, LANES), bf),
            vmem((RD * 64, LANES), f32),
            vmem((2 * KP, 384), f32),
            vmem((64 * KP, LANES), f32),
            vmem((8, 8, KP, LANES), bf),
            vmem((8, 8, KP, LANES), bf),
            vmem((4, PTILE, 2 * LANES), f32),
            vmem((4, PTILE, 2 * LANES), f32),
            vmem((8, 8, KP, LANES), bf),
            vmem((8, 8, KP, LANES), bf),
            vmem((8, 8, KP, LANES), bf),
            vmem((8, 8, KP, LANES), bf),
            dma((6,)),
            dma((17,)),
            dma((17,)),
            dma((2, 16)),
            dma((2, 16)),
            dma((16,)),
            dma((16,)),
            dma((7, 7)),
            dma((7, 7)),
        ],
        compiler_params=pltpu.CompilerParams(
            collective_id=0, has_side_effects=True, vmem_limit_bytes=60 * 1024 * 1024
        ),
    )(orbitals, counts.reshape(1, NKD), occupation, coulomb, table)


def solution(mesh):
    finer = Mesh(mesh.devices.reshape(4, 2, 16, 4), ("ka_0", "ka_1", "pts_0", "pts_1"))
    in_specs = (P(KA, None, PTS, None), P(KA), P(KA, None), P(KA, None, None, PTS))
    out_specs = P(KA, None, None, PTS)
    return jax.shard_map(local, mesh=finer, in_specs=in_specs, out_specs=out_specs, check_vma=False)
```

time: 195 us -> 67.2 us (0.34)
  Pallas kernels: 0 us -> 64.8 us
  local copies, waits for them, and re-layouts: 63.6 us -> 2.17 us
  waiting for transfers between devices: 45.5 us -> 0 us
  blocking collectives: 26.3 us -> 0 us
  starting transfers between devices: 25.9 us -> 0 us
  matrix products: 17.1 us -> 0 us
  between operations: 13.7 us -> 0.01 us
    pallas_call x0 -> x1, Pallas kernels: none -> 64.8 us  [local(): pl.pallas_call(kernel, out_shape=jax.ShapeDtypeStruct((NKD, 2, 64, 64), b...]
    all_gather x1 -> x0, waiting for transfers between devices: 32.4 us -> none  [gather_axes(): array = lax.all_gather(array, axis, axis=dim, tiled=True)]
    all_to_all x2 -> x0, starting transfers between devices: 25.9 us -> none  [the longest x1 14.1 us: local(): lax.all_to_all(density, KA, split_axis=3, concat_axis=0, tiled=True)]
    reshape x3 -> x0, local copies, waits for them, and re-layouts: 20.6 us -> none  [the longest x1 9.7 us: convolve(): kernel.astype(jnp.float32).reshape(KSIDE, KSIDE, KSIDE, 2, -1)]
    dot_general x13 -> x0, matrix products: 17.1 us -> none  [the longest x9 14.7 us: mesh_transform(): jnp.einsum(form, table, values, precision=lax.Precision.HIGHEST, preferre...]
    convert_element_type x3 -> x0, local copies, waits for them, and re-layouts: 15.3 us -> none  [convolve(): return (back * scale).reshape(shape).astype(jnp.bfloat16)]
    all_to_all x2 -> x0, blocking collectives: 15 us -> none  [moved_by_axis(): whole = lax.all_to_all(whole, axes[k], k, k, tiled=True)]
    all_to_all x2 -> x0, waiting for transfers between devices: 13.1 us -> none  [the longest x1 8.24 us: local(): lax.all_to_all(coulomb, KA, split_axis=3, concat_axis=0, tiled=True)]
  transfers between devices with their start and end apart: 3 -> 0, of which waited for: 3 -> 0; matrix products, arithmetic and copies ran while one was open for 12% -> 0% of each run, Pallas kernels for 0% -> 0%
where the time goes in v2:
time: 67.2 us; the launch traced here: 67 us
  Pallas kernels  64.8 us (96%)
  local copies, waits for them, and re-layouts  2.17 us (3%)
    pallas_call x1, Pallas kernels, local(): pl.pallas_call(kernel, out_shape=jax.ShapeDtypeStruct((NKD, 2, 64, 64), b...  64.8 us
    unnamed x1, local copies, waits for them, and re-layouts  2.17 us

profile of v2, /device:TPU:1, one launch (start us, length us, event | category | flops | bytes accessed | tf_op | source)
XLA Modules:
  0.0 67.0 jit_solution(15018174582644252635)
XLA Ops:
  0.0 64.8 %shard_map.55 = bf16[27,2,64,64]{3,2,1,0:T(8,128)(2,1)} custom-call(bf16[27,2,64,384]{3,2,1,0:T(8,128)(2,1)} %orb_hbm.1, s32[1,27]{1,0:T(1,128)} %bitcast.1, f32[27,384]{1,0:T(8,128)} %occ_hbm.1, bf16[27,2,64,64]{3,2,1,0:T(8,128)(2,1)} %cou_hbm.1, bf16[512,256]{1,0:T(8,128)(2,1)} %constant.2.clone.table_hbm), custom_call_target="tpu_custom_call" | custom-call | tf_op jit(solution)/shard_map/pallas_call | solution.py:367
  64.8 2.2 %copy.7 = bf16[27,2,64,64]{3,2,1,0:T(8,128)(2,1)} copy(bf16[27,2,64,64]{3,2,1,0:T(8,128)(2,1)} %shard_map.55) | data formatting | bytes 884736

commit v3 on v2

--- a/solution.py
+++ b/solution.py
@@ -25,7 +25,7 @@
 SCALE = -1.0 / float(KSIDE**6)
 
 DELTA_Y = (0, 1, 3, 2)
-STAGES = ((0, 1), (1, 2), (3, 1))
+STAGES = ((0, 3), (3, 1))
 OFFSETS = (0, -1, 1, -2, 2, -4, 4, -5, 3, -3, 5, -6, 6, 8, 7, -7)
 NEAR = {0: (1, -1, 2, -2), -4: (1, -1, 2), 4: (1, -1, -2), 8: (1, -1)}
 CUT = 80
@@ -209,10 +209,18 @@
         )
         return carry
 
-    def scatter(stage, u, o, y):
+    def scatter(stage, start, count, us):
         first_group, groups = STAGES[stage]
         base, rows = first_group * 16 * RD, groups * 16
-        spread[pl.ds(base + u * 16 + zz(o), RD, stride=rows), :] = gath[zz(o), y].astype(jnp.float32)
+
+        def one(i, carry):
+            z = lax.rem(z0 + start + i, 16)
+            for u in us:
+                y = yy(DELTA_Y[first_group + u])
+                spread[pl.ds(base + u * 16 + z, RD, stride=rows), :] = gath[z, y].astype(jnp.float32)
+            return carry
+
+        lax.fori_loop(0, count, one, 0)
 
     def dens(stage, start, stop):
         first_group, groups = STAGES[stage]
@@ -304,18 +312,14 @@
     for o in (7, -7):
         arrive(o)
     lax.fori_loop(18, NKD, turn, 0)
-    for o in OFFSETS[:8]:
-        scatter(0, 0, o, y0)
+    scatter(0, 10, 7, (0,))
     for o in (-5, 3, -3):
         pass_on(o)
-    for o in OFFSETS[8:]:
-        scatter(0, 0, o, y0)
+    scatter(0, 1, 9, (0,))
     for o in (5, -6, 6):
         pass_on(o)
     for k in range(NKD, KP):
         dense[pl.ds(k, 64, stride=KP), :] = jnp.zeros((64, LANES), jnp.float32)
-    dens(0, 0, NKD)
-    hand_over(0)
     for o in (8, 7, -7):
         pass_on(o)
 
@@ -331,22 +335,21 @@
 
     for y in range(4):
         kern(y)
-    for o in OFFSETS:
-        for u in range(2):
-            scatter(1, u, o, yy((1, 3)[u]))
+    scatter(0, 0, 16, (1, 2))
+    dens(0, 0, NKD)
+    hand_over(0)
+    for o in OFFSETS[:13]:
+        onward(o, yy(2)).wait_recv()
+    scatter(1, 10, 13, (0,))
+    for o in OFFSETS[13:]:
+        onward(o, yy(2)).wait_recv()
+    scatter(1, 7, 3, (0,))
     dens(1, 0, NKD)
     hand_over(1)
     convolve(0)
-    for o in OFFSETS:
-        onward(o, yy(2)).wait_recv()
-        scatter(2, 0, o, yy(2))
-    dens(2, 0, NKD)
-    hand_over(2)
     convolve(1)
     unlay(0)
-    convolve(2)
     unlay(1)
-    unlay(2)
 
     def finish(k, carry):
         o = spread[pl.ds(pl.multiple_of(k * 64, 64), 64), :]

time: 67.2 us -> 67.7 us (level)
  no operation moved by 1% of the time
where the time goes in v3:
time: 67.7 us; the launch traced here: 67.6 us
  Pallas kernels  65.4 us (97%)
  local copies, waits for them, and re-layouts  2.17 us (3%)
    pallas_call x1, Pallas kernels, local(): pl.pallas_call(kernel, out_shape=jax.ShapeDtypeStruct((NKD, 2, 64, 64), b...  65.4 us
    unnamed x1, local copies, waits for them, and re-layouts  2.17 us

profile of v3, /device:TPU:1, one launch (start us, length us, event | category | flops | bytes accessed | tf_op | source)
XLA Modules:
  0.0 67.6 jit_solution(10074829861485668064)
XLA Ops:
  0.0 65.4 %shard_map.55 = bf16[27,2,64,64]{3,2,1,0:T(8,128)(2,1)} custom-call(bf16[27,2,64,384]{3,2,1,0:T(8,128)(2,1)} %orb_hbm.1, s32[1,27]{1,0:T(1,128)} %bitcast.1, f32[27,384]{1,0:T(8,128)} %occ_hbm.1, bf16[27,2,64,64]{3,2,1,0:T(8,128)(2,1)} %cou_hbm.1, bf16[512,256]{1,0:T(8,128)(2,1)} %constant.2.clone.table_hbm), custom_call_target="tpu_custom_call" | custom-call | tf_op jit(solution)/shard_map/pallas_call | solution.py:370
  65.4 2.2 %copy.7 = bf16[27,2,64,64]{3,2,1,0:T(8,128)(2,1)} copy(bf16[27,2,64,64]{3,2,1,0:T(8,128)(2,1)} %shard_map.55) | data formatting | bytes 884736

commit v4 on v2

--- a/solution.py
+++ b/solution.py
@@ -183,7 +183,7 @@
         dense[pl.ds(k, 64, stride=KP), :] = pair
         return carry
 
-    lax.fori_loop(0, NKD, lay, 0)
+    lax.fori_loop(0, NKD, lay, 0, unroll=9)
     vsend[...] = dense[...].astype(jnp.bfloat16).reshape(8, 8, KP, LANES)
 
     def move(stage, src, dst, d):
@@ -209,10 +209,18 @@
         )
         return carry
 
-    def scatter(stage, u, o, y):
+    def scatter(stage, start, count):
         first_group, groups = STAGES[stage]
         base, rows = first_group * 16 * RD, groups * 16
-        spread[pl.ds(base + u * 16 + zz(o), RD, stride=rows), :] = gath[zz(o), y].astype(jnp.float32)
+
+        def one(i, carry):
+            z = lax.rem(z0 + start + i, 16)
+            for u in range(groups):
+                y = yy(DELTA_Y[first_group + u])
+                spread[pl.ds(base + u * 16 + z, RD, stride=rows), :] = gath[z, y].astype(jnp.float32)
+            return carry
+
+        lax.fori_loop(0, count, one, 0)
 
     def dens(stage, start, stop):
         first_group, groups = STAGES[stage]
@@ -229,7 +237,7 @@
             dense[pl.ds(first_group * 16 * KP + k, rows, stride=KP), :] = d
             return carry
 
-        lax.fori_loop(start, stop, one, 0, unroll=3)
+        lax.fori_loop(start, stop, one, 0, unroll=9)
 
     def hand_over(stage):
         first_group, groups = STAGES[stage]
@@ -279,7 +287,7 @@
                     spread[pl.ds(r, KP, stride=64), :] = orecv[a, 2 * u + i].astype(jnp.float32)
             return carry
 
-        lax.fori_loop(0, 8, one, 0)
+        lax.fori_loop(0, 8, one, 0, unroll=2)
 
     for o in (-1, 1, -2, 2):
         arrive(o)
@@ -289,7 +297,7 @@
         go(chain(o))
         near(o)
     loads[4].wait()
-    lax.fori_loop(0, 9, turn, 0)
+    lax.fori_loop(0, 9, turn, 0, unroll=3)
     for o in (-5, 3, -3, 5, -6, 6):
         arrive(o)
     for o in (-1, 1, -2, 2):
@@ -298,18 +306,16 @@
         chained(o).wait_recv()
     sides(8)
     near(8)
-    lax.fori_loop(9, 18, turn, 0)
+    lax.fori_loop(9, 18, turn, 0, unroll=3)
     for o in (-4, 4):
         pass_on(o)
     for o in (7, -7):
         arrive(o)
-    lax.fori_loop(18, NKD, turn, 0)
-    for o in OFFSETS[:8]:
-        scatter(0, 0, o, y0)
+    lax.fori_loop(18, NKD, turn, 0, unroll=3)
+    scatter(0, 10, 7)
     for o in (-5, 3, -3):
         pass_on(o)
-    for o in OFFSETS[8:]:
-        scatter(0, 0, o, y0)
+    scatter(0, 1, 9)
     for o in (5, -6, 6):
         pass_on(o)
     for k in range(NKD, KP):
@@ -331,15 +337,16 @@
 
     for y in range(4):
         kern(y)
-    for o in OFFSETS:
-        for u in range(2):
-            scatter(1, u, o, yy((1, 3)[u]))
+    scatter(1, 0, 16)
     dens(1, 0, NKD)
     hand_over(1)
     convolve(0)
-    for o in OFFSETS:
+    for o in OFFSETS[:13]:
         onward(o, yy(2)).wait_recv()
-        scatter(2, 0, o, yy(2))
+    scatter(2, 10, 13)
+    for o in OFFSETS[13:]:
+        onward(o, yy(2)).wait_recv()
+    scatter(2, 7, 3)
     dens(2, 0, NKD)
     hand_over(2)
     convolve(1)
@@ -354,7 +361,7 @@
         out_ref[k, 1] = swap(o)[:, :HALF].astype(jnp.bfloat16)
         return carry
 
-    lax.fori_loop(0, NKD, finish, 0)
+    lax.fori_loop(0, NKD, finish, 0, unroll=9)
     for copy in sent:
         copy.wait_send()
 

time: 67.2 us -> 64.2 us (0.955)
  Pallas kernels: 64.8 us -> 61.9 us
    pallas_call x1, Pallas kernels: 64.8 us -> 61.9 us  [local(): pl.pallas_call(kernel, out_shape=jax.ShapeDtypeStruct((NKD, 2, 64, 64), b...]
where the time goes in v4:
time: 64.2 us; the launch traced here: 64 us
  Pallas kernels  61.9 us (96%)
  local copies, waits for them, and re-layouts  2.17 us (3%)
    pallas_call x1, Pallas kernels, local(): pl.pallas_call(kernel, out_shape=jax.ShapeDtypeStruct((NKD, 2, 64, 64), b...  61.9 us
    unnamed x1, local copies, waits for them, and re-layouts  2.17 us

profile of v4, /device:TPU:1, one launch (start us, length us, event | category | flops | bytes accessed | tf_op | source)
XLA Modules:
  0.0 64.0 jit_solution(13944895655075711145)
XLA Ops:
  0.0 61.9 %shard_map.55 = bf16[27,2,64,64]{3,2,1,0:T(8,128)(2,1)} custom-call(bf16[27,2,64,384]{3,2,1,0:T(8,128)(2,1)} %orb_hbm.1, s32[1,27]{1,0:T(1,128)} %bitcast.1, f32[27,384]{1,0:T(8,128)} %occ_hbm.1, bf16[27,2,64,64]{3,2,1,0:T(8,128)(2,1)} %cou_hbm.1, bf16[512,256]{1,0:T(8,128)(2,1)} %constant.2.clone.table_hbm), custom_call_target="tpu_custom_call" | custom-call | tf_op jit(solution)/shard_map/pallas_call | solution.py:374
  61.9 2.2 %copy.7 = bf16[27,2,64,64]{3,2,1,0:T(8,128)(2,1)} copy(bf16[27,2,64,64]{3,2,1,0:T(8,128)(2,1)} %shard_map.55) | data formatting | bytes 884736

commit v5 on v4

--- a/solution.py
+++ b/solution.py
@@ -237,7 +237,7 @@
             dense[pl.ds(first_group * 16 * KP + k, rows, stride=KP), :] = d
             return carry
 
-        lax.fori_loop(start, stop, one, 0, unroll=9)
+        lax.fori_loop(start, stop, one, 0, unroll=27)
 
     def hand_over(stage):
         first_group, groups = STAGES[stage]
@@ -287,7 +287,7 @@
                     spread[pl.ds(r, KP, stride=64), :] = orecv[a, 2 * u + i].astype(jnp.float32)
             return carry
 
-        lax.fori_loop(0, 8, one, 0, unroll=2)
+        lax.fori_loop(0, 8, one, 0, unroll=4)
 
     for o in (-1, 1, -2, 2):
         arrive(o)
@@ -297,7 +297,7 @@
         go(chain(o))
         near(o)
     loads[4].wait()
-    lax.fori_loop(0, 9, turn, 0, unroll=3)
+    lax.fori_loop(0, 9, turn, 0, unroll=9)
     for o in (-5, 3, -3, 5, -6, 6):
         arrive(o)
     for o in (-1, 1, -2, 2):
@@ -306,12 +306,12 @@
         chained(o).wait_recv()
     sides(8)
     near(8)
-    lax.fori_loop(9, 18, turn, 0, unroll=3)
+    lax.fori_loop(9, 18, turn, 0, unroll=9)
     for o in (-4, 4):
         pass_on(o)
     for o in (7, -7):
         arrive(o)
-    lax.fori_loop(18, NKD, turn, 0, unroll=3)
+    lax.fori_loop(18, NKD, turn, 0, unroll=9)
     scatter(0, 10, 7)
     for o in (-5, 3, -3):
         pass_on(o)

time: 64.2 us -> 63.7 us (level)
  no operation moved by 1% of the time
where the time goes in v5:
time: 63.7 us; the launch traced here: 63.5 us
  Pallas kernels  61.3 us (96%)
  local copies, waits for them, and re-layouts  2.17 us (3%)
    pallas_call x1, Pallas kernels, local(): pl.pallas_call(kernel, out_shape=jax.ShapeDtypeStruct((NKD, 2, 64, 64), b...  61.3 us
    unnamed x1, local copies, waits for them, and re-layouts  2.17 us

profile of v5, /device:TPU:1, one launch (start us, length us, event | category | flops | bytes accessed | tf_op | source)
XLA Modules:
  0.0 63.5 jit_solution(3016978474281615831)
XLA Ops:
  0.0 61.3 %shard_map.55 = bf16[27,2,64,64]{3,2,1,0:T(8,128)(2,1)} custom-call(bf16[27,2,64,384]{3,2,1,0:T(8,128)(2,1)} %orb_hbm.1, s32[1,27]{1,0:T(1,128)} %bitcast.1, f32[27,384]{1,0:T(8,128)} %occ_hbm.1, bf16[27,2,64,64]{3,2,1,0:T(8,128)(2,1)} %cou_hbm.1, bf16[512,256]{1,0:T(8,128)(2,1)} %constant.2.clone.table_hbm), custom_call_target="tpu_custom_call" | custom-call | tf_op jit(solution)/shard_map/pallas_call | solution.py:374
  61.3 2.2 %copy.7 = bf16[27,2,64,64]{3,2,1,0:T(8,128)(2,1)} copy(bf16[27,2,64,64]{3,2,1,0:T(8,128)(2,1)} %shard_map.55) | data formatting | bytes 884736
